TPU v7x, 32 devices: a whole 2x2x4 slice. The times are simulated.
32 devices in a mesh: grp: 2 (over y), freq: 4 (over z), shot: 2 (over x), rcv: 2 (over core).
Axes of the slice: x: 2, y: 2, z: 4, core: 2. Of those that a mesh axis runs over, the one named last changes fastest.
Arguments:
- data: bfloat16 [2, 256, 32, 4096], P(None, 'freq', ('grp', 'shot'), 'rcv'), parts along dimension 2, may hold values from -6 to 6
- estimate: bfloat16 [2, 256, 32, 4096], P(None, 'freq', ('grp', 'shot'), 'rcv'), parts along dimension 2, may hold values from -0.09375 to 0.09375
- window_data: bfloat16 [2, 256, 32, 16], P(None, 'freq', ('grp', 'shot')), parts along dimension 2, may hold values from -6 to 6
- wavelet: float32 [2, 512], P(None, ('grp', 'freq')), parts along dimension 1, may hold values from -24 to 24
- positions: int32 [32], P(('grp', 'shot')), parts along dimension 0, may hold values from 0 to 4095
- bins: int32 [512], P('grp'), parts along dimension 0, may hold values from 0 to 399
- threshold: int32 [2], P('grp'), parts along dimension 0, may hold values from 8 to 40
- step: float32 [2], P('grp'), parts along dimension 0, may hold values from 0.25 to 1
Outputs:
- primaries: bfloat16 [1024, 32, 4096], P('freq', ('grp', 'shot'), 'rcv'), parts along dimension 1
There are 2 independent parts, one for each index of `grp`. A program takes and returns all parts, laid end to end along the dimension named above; each array names one. Nothing has to cross between parts.
All inputs are finite; a program needn't handle non-finite values.
Results may differ from a plain program's by a relative error of at most 0.0059.
The roundings to bfloat16 on the way count: a program that leaves them out, or rounds other values in their place, can miss the bound.
Values may be sent and summed in bfloat16 or wider, within the bound.
A program may use at most 64 MiB of HBM per device.

v0:
```python
from functools import partial
import math

import jax
import jax.numpy as jnp
from jax import lax
from jax.sharding import PartitionSpec as P

NF = 256
RCV = 4096
NT = 1024


def make_down(lines, spots, wavelet, offset):
    width = lines.shape[3]
    columns = offset + lax.iota(jnp.int32, width)
    select = (columns[None, None, :] == spots[None, :, None]).astype(jnp.float32)
    down_re = (wavelet[0][:, None, None] * select - lines[0].astype(jnp.float32)).astype(
        jnp.bfloat16
    )
    down_im = (wavelet[1][:, None, None] * select - lines[1].astype(jnp.float32)).astype(
        jnp.bfloat16
    )
    return (down_re, down_im)


def body(data, estimate, window_data, wavelet, positions, bins, threshold, step):
    product = partial(jnp.einsum, preferred_element_type=jnp.float32)
    offset = lax.axis_index("rcv") * data.shape[3]
    shots_all = data.shape[2] * lax.axis_size("shot")
    norm = 1.0 / math.sqrt(shots_all * RCV)
    lines, spots = (
        lax.all_gather(data, "shot", axis=2, tiled=True),
        lax.all_gather(positions, "shot", axis=0, tiled=True),
    )
    down_re, down_im = make_down(lines, spots, wavelet, offset)
    rows_re = estimate[0]
    rows_im = estimate[1]
    model_re = product("frc,fsc->frs", rows_re, down_re) - product("frc,fsc->frs", rows_im, down_im)
    model_im = product("frc,fsc->frs", rows_re, down_im) + product("frc,fsc->frs", rows_im, down_re)
    model_re, model_im = lax.psum((model_re, model_im), "rcv")
    err_re = (window_data[0].astype(jnp.float32) - model_re).astype(jnp.bfloat16)
    err_im = (window_data[1].astype(jnp.float32) - model_im).astype(jnp.bfloat16)
    grad_re = product("frs,fsc->frc", err_re, down_re) + product("frs,fsc->frc", err_im, down_im)
    grad_im = product("frs,fsc->frc", err_im, down_re) - product("frs,fsc->frc", err_re, down_im)
    step_size = step[0]
    upd_re = (estimate[0].astype(jnp.float32) - step_size * (grad_re * norm)).astype(jnp.bfloat16)
    upd_im = (estimate[1].astype(jnp.float32) - step_size * (grad_im * norm)).astype(jnp.bfloat16)
    updated = jnp.stack([upd_re, upd_im], axis=0)
    n_freq = bins.shape[0]
    times = lax.iota(jnp.int32, NT)
    phase = bins[:, None] * times[None, :] % NT
    angle = 2.0 * math.pi / NT * phase.astype(jnp.float32)
    table = jnp.concatenate([jnp.cos(angle), -jnp.sin(angle)], axis=0).astype(jnp.bfloat16)
    level = threshold[0].astype(jnp.float32) / 64.0
    amplitude = math.sqrt(RCV / NF)
    piece = lax.all_to_all(updated, "freq", split_axis=3, concat_axis=1, tiled=True)
    row_count = piece.shape[2]
    col_count = piece.shape[3]
    stacked = piece.reshape(2 * n_freq, row_count * col_count)
    trace = (
        lax.dot_general(
            table, stacked, (((0,), (0,)), ((), ())), preferred_element_type=jnp.float32
        )
        * amplitude
    )
    sparse = (jnp.sign(trace) * jnp.maximum(jnp.abs(trace) - level, 0.0)).astype(jnp.bfloat16)
    sparse = sparse.reshape(NT, row_count, col_count)
    return lax.all_to_all(sparse, "freq", split_axis=0, concat_axis=2, tiled=True)


def solution(mesh):
    return jax.shard_map(
        body,
        mesh=mesh,
        in_specs=(
            P(None, "freq", ("grp", "shot"), "rcv"),
            P(None, "freq", ("grp", "shot"), "rcv"),
            P(None, "freq", ("grp", "shot"), None),
            P(None, ("grp", "freq")),
            P(("grp", "shot")),
            P("grp"),
            P("grp"),
            P("grp"),
        ),
        out_specs=P("freq", ("grp", "shot"), "rcv"),
        check_vma=False,
    )
```

profile of v0, /device:TPU:0, one launch (start us, length us, event | category | flops | bytes accessed | tf_op | source)
XLA Modules:
  0.0 535.6 jit_solution(10995999869594317697)
XLA Ops:
  6.5 0.7 all-gather.2.cloned.1.call-update
  7.3 0.6 dynamic-slice
  8.6 0.2 dynamic-update-slice
  8.8 5.2 all-reduce
  14.1 101.5 %all-gather.2.cloned.1.call-done = bf16[2,64,16,2048]{3,2,1,0:T(8,128)(2,1)} async-done(((bf16[2,64,8,2048]{3,2,1,0:T(8,128)(2,1)}), bf16[2,64,16,2048]{3,2,1,0:T(8,128)(2,1)}) %all-gather.2.cloned.1.call-update) | async-done | bytes 8388624 | tf_op jit(solution)/shard_map/all_gather | solution.py:33
  115.6 5.3 fusion
  121.0 1.6 fusion.6
  122.6 1.6 fusion.4
  124.1 2.3 fusion.19
  126.4 1.9 fusion.25
  128.5 0.1 copy.27
  129.3 18.0 %all-reduce.4.cloned.1.call-done = (f32[64,8,16]{2,1,0:T(8,128)}, f32[64,8,16]{2,1,0:T(8,128)}) async-done(((f32[64,8,16]{2,1,0:T(8,128)}, f32[64,8,16]{2,1,0:T(8,128)}), (f32[64,8,16]{2,1,0:T(8,128)}, f32[64,8,16]{2,1,0:T(8,128)})) %all-reduce.4.cloned.1.call-update) | async-done | bytes 65552 | tf_op jit(solution)/shard_map/psum | solution.py:41
  147.3 3.1 fusion.41
  150.4 0.4 copy-done.3
  150.9 0.7 fusion.43
  151.6 1.5 copy-done.1
  153.1 1.3 copy-done.5
  154.3 1.0 fusion.2
  155.3 1.0 fusion.3
  156.3 2.3 pad_maximum_fusion
  158.6 13.2 %copy.23 = bf16[2,64,8,2048]{1,2,0,3:T(8,128)(2,1)} copy(bf16[2,64,8,2048]{3,2,1,0:T(8,128)(2,1)} %pad_maximum_fusion) | data formatting | bytes 8388608 | tf_op jit(solution)/shard_map/stack | solution.py:49
  171.8 9.6 %reshape.71 = bf16[4,2,262144]{2,1,0:T(2,128)(2,1)} reshape(bf16[2048,2,8,64]{3,2,1,0:T(8,128)(2,1)} %bitcast.77) | data formatting | bytes 8388608
  181.4 5.0 all-to-all-start
  187.1 4.9 cosine_convert_fusion
  191.9 88.4 %all-to-all-done = bf16[4,2,262144]{2,1,0:T(2,128)(2,1)} async-done(((bf16[4,2,262144]{2,1,0:T(2,128)(2,1)}), bf16[4,2,262144]{2,1,0:T(2,128)(2,1)}, u32[]{:S(2)}, u32[]{:S(2)}) %all-to-all-start) | async-done | bytes 4194336 | tf_op jit(solution)/shard_map/all_to_all | solution.py:57
  280.3 9.3 %reshape.72 = bf16[2048,2,8,64]{3,2,1,0:T(8,128)(2,1)} reshape(bf16[4,2,262144]{2,1,0:T(2,128)(2,1)} %all-to-all-done) | data formatting | bytes 8388608
  289.6 12.0 %copy.24 = bf16[2,64,8,4,512]{4,2,1,3,0:T(8,128)(2,1)} copy(bf16[2,64,8,4,512]{1,2,0,4,3:T(8,128)(2,1)} %bitcast.78) | data formatting | bytes 8388608 | tf_op jit(solution)/shard_map/all_to_all | solution.py:57
  301.6 4.4 copy.28
  306.0 12.1 %multiply_convert_fusion = bf16[1024,4096]{1,0:T(8,128)(2,1)} fusion(bf16[512,4096]{1,0:T(8,128)(2,1)S(1)} %bitcast.83, f32[]{:T(128)} %bitcast.16, bf16[256,1024]{1,0:T(8,128)(2,1)S(1)} %get-tuple-element.12, bf16[256,1024]{1,0:T(8,128)(2,1)S(1)} %get-tuple-element.11), kind=kOutput, calls=%fused_computation | convolution fusion | flops 4326424576 | bytes 13631492 | tf_op jit(solution)/shard_map/dot_general | solution.py:62
  318.1 12.2 %copy.29 = bf16[128,8,8,512]{3,2,1,0:T(8,128)(2,1)} copy(bf16[128,8,8,512]{3,1,2,0:T(8,128)(2,1)} %bitcast.82) | data formatting | bytes 16777216
  330.3 190.4 %all_to_all.33 = bf16[1024,8,512]{2,1,0:T(8,128)(2,1)} all-to-all(bf16[1024,8,512]{2,1,0:T(8,128)(2,1)} %bitcast.79), channel_id=1, replica_groups=mesh['grp'=2,'freq'=4,'shot'=2,'rcv'=2] {'freq'}, dimensions={0} | all-to-all | bytes 16777216 | tf_op jit(solution)/shard_map/all_to_all | solution.py:69
  520.7 8.1 %copy.25 = bf16[4,256,8,512]{3,2,0,1:T(8,128)(2,1)} copy(bf16[4,256,8,512]{3,2,1,0:T(8,128)(2,1)} %bitcast.80) | data formatting | bytes 16777216 | tf_op jit(solution)/shard_map/all_to_all | solution.py:69
  (32 shorter events, 0.4 us)
Async XLA Ops:
  6.5 0.8 copy-start.12
  6.5 2.0 copy-start.11
  6.5 7.5 %copy-start.10 = (f32[2,64]{1,0:T(2,128)S(1)}, f32[2,64]{1,0:T(2,128)}, u32[]{:S(2)}) copy-start(f32[2,64]{1,0:T(2,128)} %param.11) | copy-start | bytes 1540
  6.5 109.1 %all-gather.2.cloned.1.call-start = ((), (), s32[]{:S(2)}) async-start(), calls=%async_computation.2 | async-start | bytes 12582912 | tf_op jit(solution)/shard_map/all_gather | solution.py:33
  7.3 140.1 %all-reduce.4.cloned.1.call-start = ((), (), s32[]{:S(2)}) async-start(), calls=%async_computation.3 | async-start | bytes 1048576 | tf_op jit(solution)/shard_map/psum | solution.py:41
  115.6 5.3 copy-start.4
  121.0 3.2 copy-start.2
  121.0 5.5 %copy-start = (bf16[64,16,2048]{2,1,0:T(8,128)(2,1)}, bf16[64,16,2048]{2,1,0:T(8,128)(2,1)S(1)}, u32[]{:S(2)}) copy-start(bf16[64,16,2048]{2,1,0:T(8,128)(2,1)S(1)} %get-tuple-element.7) | copy-start | bytes 12582916
  126.4 1.9 copy-start.8
  147.3 3.5 copy-start.3
  147.3 3.5 copy-start.7
  150.9 2.2 copy-start.1
  150.9 3.5 copy-start.5
  154.3 1.0 copy-start.6
  181.4 5.7 %copy-start.9 = (s32[256]{0:T(256)S(1)}, s32[256]{0:T(256)}, u32[]{:S(2)}) copy-start(s32[256]{0:T(256)} %param.13) | copy-start | bytes 3076
  181.4 99.0 %all-to-all-start = ((bf16[4,2,262144]{2,1,0:T(2,128)(2,1)}), bf16[4,2,262144]{2,1,0:T(2,128)(2,1)}, u32[]{:S(2)}, u32[]{:S(2)}) async-start(bf16[4,2,262144]{2,1,0:T(2,128)(2,1)} %reshape.71), calls=%async_computation | async-start | bytes 8388608 | tf_op jit(solution)/shard_map/all_to_all | solution.py:57
Sparse Core Ops, SparseCore 0:
  8.9 106.6 all-gather.1
  128.5 18.7 all-reduce.3
where the time goes:
time: 537 us; the launch traced here: 536 us
  waiting for transfers between devices  209 us (39%)
  blocking collectives  196 us (36%)
  local copies, waits for them, and re-layouts  73.1 us (14%)
  matrix products  25.2 us (5%)
  between operations  15.5 us (3%)
  other arithmetic  12.6 us (2%)
    all_to_all x1, blocking collectives, body(): lax.all_to_all(sparse, 'freq', split_axis=0, concat_axis=2, tiled=True)  190 us
    all_gather x1, waiting for transfers between devices, body(): lax.all_gather(data, 'shot', axis=2, tiled=True)  102 us
    all_to_all x1, waiting for transfers between devices, body(): lax.all_to_all(updated, 'freq', split_axis=3, concat_axis=1, tiled=True)  88.4 us
    unnamed x35, local copies, waits for them, and re-layouts  39.8 us
    psum x1, waiting for transfers between devices, body(): model_re, model_im = lax.psum((model_re, model_im), 'rcv')  18 us
    another operation x1, local copies, waits for them, and re-layouts, body(): updated = jnp.stack([upd_re, upd_im], axis=0)  13.2 us
    dot_general x1, matrix products, body(): lax.dot_general(table, stacked, (((0,), (0,)), ((), ())), preferred_eleme...  12.1 us
    all_to_all x1, local copies, waits for them, and re-layouts, body(): lax.all_to_all(updated, 'freq', split_axis=3, concat_axis=1, tiled=True)  12 us
  transfers between devices with their start and end apart: 3, of which 3 were waited for; matrix products, arithmetic and copies ran while one was open for 1% of the time, Pallas kernels for 0%

commit v1 on v0

v1 whole, which is shorter than its diff:
```python
from functools import partial
import math

import jax
import jax.numpy as jnp
from jax import lax
from jax.experimental import pallas as pl
from jax.experimental.pallas import tpu as pltpu
from jax.sharding import PartitionSpec as P

NF = 256
RCV = 4096
NT = 1024
FC = 8
MESH = pl.DeviceIdType.MESH


def iota(shape, dim):
    return lax.broadcasted_iota(jnp.int32, shape, dim)


def update_kernel(
    nx, nz, nchunk, rows, lines, norm,
    data, est, win, wav, pos, step, out,
    down, est_p, upd, mod_mine, mod_other,
    x_send, x_recv, c_send, c_recv, r_send, r_recv, l_send, l_recv, own_sem,
):
    mx = lax.axis_index("shot")
    mz = lax.axis_index("freq")
    mc = lax.axis_index("rcv")
    width = data.shape[2]
    fl = FC * lines
    fi = FC * rows

    barrier = pltpu.get_barrier_semaphore()
    for d in range(1, nx):
        pl.semaphore_signal(
            barrier, inc=1, device_id={"shot": lax.rem(mx + d, nx)}, device_id_type=MESH
        )
    pl.semaphore_signal(barrier, inc=1, device_id={"rcv": 1 - mc}, device_id_type=MESH)

    @pl.when(mz > 0)
    def _():
        pl.semaphore_signal(barrier, inc=1, device_id={"freq": mz - 1}, device_id_type=MESH)

    @pl.when(mz < nz - 1)
    def _():
        pl.semaphore_signal(barrier, inc=1, device_id={"freq": mz + 1}, device_id_type=MESH)

    ends = (mz > 0).astype(jnp.int32) + (mz < nz - 1).astype(jnp.int32)
    pl.semaphore_wait(barrier, nx + ends)

    def x_copy(d, k):
        piece = down.at[k, :, pl.ds(mx * fl, fl)]
        return pltpu.make_async_remote_copy(
            src_ref=piece, dst_ref=piece,
            send_sem=x_send.at[d, k], recv_sem=x_recv.at[d, k],
            device_id={"shot": lax.rem(mx + d, nx)}, device_id_type=MESH,
        )

    def c_copy(k):
        return pltpu.make_async_remote_copy(
            src_ref=mod_mine.at[k], dst_ref=mod_other.at[k],
            send_sem=c_send.at[k], recv_sem=c_recv.at[k],
            device_id={"rcv": 1 - mc}, device_id_type=MESH,
        )

    def z_copy(src, slot, k, way):
        send, recv = (r_send, r_recv) if way > 0 else (l_send, l_recv)
        return pltpu.make_async_remote_copy(
            src_ref=src, dst_ref=out.at[slot, k],
            send_sem=send.at[slot, k], recv_sem=recv.at[slot, k],
            device_id={"freq": mz + way}, device_id_type=MESH,
        )

    def own_copy(k):
        return pltpu.make_async_copy(upd.at[k], out.at[mz, k], own_sem.at[k])

    column = mc * width + iota((lines, width), 1)
    select = (column == pos[:, :]).astype(jnp.float32)

    def make_down(k, carry):
        for c in range(2):
            parts = []
            lines_k = data[c, pl.ds(pl.multiple_of(k * fl, fl), fl)].astype(jnp.float32)
            for f in range(FC):
                w = wav[c, k * FC + f]
                parts.append(w * select - lines_k[f * lines:(f + 1) * lines])
            down[k, c, pl.ds(pl.multiple_of(mx * fl, fl), fl)] = jnp.concatenate(
                parts, axis=0
            ).astype(jnp.bfloat16)
        for d in range(1, nx):
            x_copy(d, k).start()
        return carry

    lax.fori_loop(0, nchunk, make_down, 0)

    n = 2 * fi
    dst, src = iota((n, n), 0), iota((n, n), 1)
    want = (dst // FC % 2) * fi + (dst % FC) * rows + dst // (2 * FC)
    perm = (src == want).astype(jnp.bfloat16)

    def chunk_of(ref, k):
        part = pl.ds(pl.multiple_of(k * fi, fi), fi)
        return jnp.concatenate([ref[0, part], ref[1, part]], axis=0)

    def permute(k, carry):
        est_p[k] = jnp.dot(
            perm, chunk_of(est, k), preferred_element_type=jnp.float32
        ).astype(jnp.bfloat16)
        return carry

    lax.fori_loop(0, nchunk, permute, 0)

    cols = nx * fl
    shots = win.shape[2]
    s_row, s_col = iota((shots, cols), 0), iota((shots, cols), 1)
    spread = (s_row == (s_col // fl) * lines + s_col % lines).astype(jnp.bfloat16)
    shape3 = (rows, FC, cols)
    same = iota(shape3, 1) == iota(shape3, 2) % fl // lines
    scale = step[0]

    def model(k):
        for d in range(1, nx):
            here = down.at[k, :, pl.ds(lax.rem(mx + nx - d, nx) * fl, fl)]
            pltpu.make_async_remote_copy(
                src_ref=here, dst_ref=here,
                send_sem=x_send.at[d, k], recv_sem=x_recv.at[d, k],
                device_id={"shot": lax.rem(mx + d, nx)}, device_id_type=MESH,
            ).wait_recv()
        lines_k = down[k].reshape(2 * cols, width)
        m = lax.dot_general(
            est_p[k], lines_k, (((1,), (1,)), ((), ())), preferred_element_type=jnp.float32
        ).reshape(rows, 2, FC, 2 * cols)
        mod_mine[k, 0] = m[:, 0, :, :cols] - m[:, 1, :, cols:]
        mod_mine[k, 1] = m[:, 0, :, cols:] + m[:, 1, :, :cols]
        c_copy(k).start()

    def update(k):
        c_copy(k).wait_recv()
        total_re = mod_mine[k, 0] + mod_other[k, 0]
        total_im = mod_mine[k, 1] + mod_other[k, 1]
        w = jnp.dot(perm, chunk_of(win, k), preferred_element_type=jnp.float32).astype(jnp.bfloat16)
        w = jnp.dot(w, spread, preferred_element_type=jnp.float32).reshape(rows, 2, FC, cols)
        e_re = jnp.where(same, w[:, 0] - total_re, 0.0)
        e_im = jnp.where(same, w[:, 1] - total_im, 0.0)
        e = jnp.stack(
            [jnp.concatenate([e_re, e_im], axis=2), jnp.concatenate([e_im, -e_re], axis=2)], axis=1
        ).reshape(n, 2 * cols).astype(jnp.bfloat16)
        grad = jnp.dot(e, down[k].reshape(2 * cols, width), preferred_element_type=jnp.float32)
        upd[k] = (est_p[k].astype(jnp.float32) - scale * (grad * norm)).astype(jnp.bfloat16)
        own_copy(k).start()

        @pl.when(mz < nz - 1)
        def _():
            z_copy(upd.at[k], mz, k, 1).start()

        @pl.when(mz > 0)
        def _():
            z_copy(upd.at[k], mz, k, -1).start()

    def step_of(k, carry):
        @pl.when(k < nchunk)
        def _():
            model(k)

        @pl.when(k > 0)
        def _():
            update(k - 1)

        return carry

    lax.fori_loop(0, nchunk + 1, step_of, 0)

    def hop(h, carry):
        def one(k, carry):
            for way in (1, -1):
                slot = mz - way * h
                inside = (slot >= 0) & (slot < nz)
                more = (mz + way >= 0) & (mz + way < nz)

                @pl.when(inside)
                def _():
                    here = out.at[slot, k]
                    z_copy(here, slot, k, way).wait_recv()

                @pl.when(inside & more)
                def _():
                    z_copy(out.at[slot, k], slot, k, way).start()

            return carry

        return lax.fori_loop(0, nchunk, one, carry)

    lax.fori_loop(1, nz, hop, 0)

    def drain(k, carry):
        for d in range(1, nx):
            x_copy(d, k).wait_send()
        c_copy(k).wait_send()
        own_copy(k).wait()

        def hop_sent(h, carry):
            for way in (1, -1):
                slot = mz - way * h
                inside = (slot >= 0) & (slot < nz)
                more = (mz + way >= 0) & (mz + way < nz)

                @pl.when(inside & more)
                def _():
                    z_copy(upd.at[k], slot, k, way).wait_send()

            return carry

        return lax.fori_loop(0, nz, hop_sent, carry)

    lax.fori_loop(0, nchunk, drain, 0)


def trace_kernel(rows, t_group, gain, level, table, u, out, sparse):
    groups, _, width = u.shape
    part = 2 * FC
    nt = table.shape[0]
    lv = level[0]
    for i in range(rows):
        ui = u[:, i * part:(i + 1) * part, :].reshape(groups * part, width)
        tr = jnp.dot(table[...], ui, preferred_element_type=jnp.float32) * gain
        sparse[i] = (jnp.maximum(tr - lv, 0.0) + jnp.minimum(tr + lv, 0.0)).astype(jnp.bfloat16)
    n = t_group * rows
    dst, src = iota((n, n), 0), iota((n, n), 1)
    perm = (src == (dst % rows) * t_group + dst // rows).astype(jnp.bfloat16)
    for g in range(nt // t_group):
        x = sparse[:, g * t_group:(g + 1) * t_group, :].reshape(n, width)
        out[g * n:(g + 1) * n, :] = jnp.dot(
            perm, x, preferred_element_type=jnp.float32
        ).astype(jnp.bfloat16)


def body(nx, nz, data, estimate, window_data, wavelet, positions, bins, threshold, step):
    _, nf, lines, width = data.shape
    rows = estimate.shape[2]
    shots = window_data.shape[3]
    nchunk = nf // FC
    norm = 1.0 / math.sqrt(shots * RCV)
    fi, cols = FC * rows, nx * FC * lines
    vmem = pl.BlockSpec(memory_space=pltpu.VMEM)
    smem = pl.BlockSpec(memory_space=pltpu.SMEM)
    dma = pltpu.SemaphoreType.DMA
    spectra = pl.pallas_call(
        partial(update_kernel, nx, nz, nchunk, rows, lines, norm),
        out_shape=jax.ShapeDtypeStruct((nz, nchunk, 2 * fi, width), jnp.bfloat16),
        in_specs=[vmem, vmem, vmem, smem, vmem, smem],
        out_specs=pl.BlockSpec(memory_space=pl.ANY),
        scratch_shapes=[
            pltpu.VMEM((nchunk, 2, cols, width), jnp.bfloat16),
            pltpu.VMEM((nchunk, 2 * fi, width), jnp.bfloat16),
            pltpu.VMEM((nchunk, 2 * fi, width), jnp.bfloat16),
            pltpu.VMEM((nchunk, 2, rows, FC, cols), jnp.float32),
            pltpu.VMEM((nchunk, 2, rows, FC, cols), jnp.float32),
            dma((nx, nchunk)), dma((nx, nchunk)),
            dma((nchunk,)), dma((nchunk,)),
            dma((nz, nchunk)), dma((nz, nchunk)),
            dma((nz, nchunk)), dma((nz, nchunk)),
            dma((nchunk,)),
        ],
        compiler_params=pltpu.CompilerParams(
            collective_id=0, has_side_effects=True, vmem_limit_bytes=56 << 20
        ),
        name="update",
    )(
        data.reshape(2, nf * lines, width),
        estimate.reshape(2, nf * rows, width),
        window_data.reshape(2, nf * rows, shots),
        wavelet,
        positions[:, None],
        step,
    )
    nt = NT // nz
    times = lax.axis_index("freq") * nt + lax.iota(jnp.int32, nt)
    phase = times[:, None] * bins[None, :] % NT
    angle = 2.0 * math.pi / NT * phase.astype(jnp.float32)
    table = jnp.stack([jnp.cos(angle), -jnp.sin(angle)], axis=1).astype(jnp.bfloat16)
    table = table.reshape(nt, 2, nz * nchunk, FC).transpose(0, 2, 1, 3).reshape(nt, 2 * nz * nf)
    level = threshold.astype(jnp.float32) / 64.0
    block = 256
    groups = nz * nchunk
    traces = pl.pallas_call(
        partial(trace_kernel, rows, 32, math.sqrt(RCV / NF)),
        out_shape=jax.ShapeDtypeStruct((nt * rows, width), jnp.bfloat16),
        grid=(width // block,),
        in_specs=[
            smem,
            pl.BlockSpec((nt, 2 * nz * nf), lambda j: (0, 0)),
            pl.BlockSpec((groups, 2 * fi, block), lambda j: (0, 0, j)),
        ],
        out_specs=pl.BlockSpec((nt * rows, block), lambda j: (0, j)),
        scratch_shapes=[pltpu.VMEM((rows, nt, block), jnp.bfloat16)],
        compiler_params=pltpu.CompilerParams(vmem_limit_bytes=40 << 20),
        name="traces",
    )(level, table, spectra.reshape(groups, 2 * fi, width))
    return traces.reshape(nt, rows, width)


def solution(mesh):
    return jax.shard_map(
        partial(body, mesh.shape["shot"], mesh.shape["freq"]),
        mesh=mesh,
        in_specs=(
            P(None, "freq", ("grp", "shot"), "rcv"),
            P(None, "freq", ("grp", "shot"), "rcv"),
            P(None, "freq", ("grp", "shot"), None),
            P(None, ("grp", "freq")),
            P(("grp", "shot")),
            P("grp"),
            P("grp"),
            P("grp"),
        ),
        out_specs=P("freq", ("grp", "shot"), "rcv"),
        check_vma=False,
    )
```

time: 537 us -> 327 us (0.61)
  Pallas kernels: 0 us -> 320 us
  waiting for transfers between devices: 209 us -> 0 us
  blocking collectives: 196 us -> 0 us
  local copies, waits for them, and re-layouts: 73.1 us -> 3.93 us
  matrix products: 25.2 us -> 0 us
  between operations: 15.5 us -> 1.34 us
  other arithmetic: 12.6 us -> 1.27 us
    pallas_call x0 -> x2, Pallas kernels: none -> 320 us  [the longest x1 306 us: body(): pl.pallas_call(partial(update_kernel, nx, nz, nchunk, rows, lines, norm),...]
    all_to_all x1 -> x0, blocking collectives: 190 us -> none  [body(): lax.all_to_all(sparse, 'freq', split_axis=0, concat_axis=2, tiled=True)]
    all_gather x1 -> x0, waiting for transfers between devices: 102 us -> none  [body(): lax.all_gather(data, 'shot', axis=2, tiled=True)]
    all_to_all x1 -> x0, waiting for transfers between devices: 88.4 us -> none  [body(): lax.all_to_all(updated, 'freq', split_axis=3, concat_axis=1, tiled=True)]
    unnamed x35 -> x1, local copies, waits for them, and re-layouts: 39.8 us -> 1.71 us
    dot_general x9 -> x0, matrix products: 25.2 us -> none  [the longest x1 12.1 us: body(): lax.dot_general(table, stacked, (((0,), (0,)), ((), ())), preferred_eleme...]
    all_to_all x2 -> x0, local copies, waits for them, and re-layouts: 20.1 us -> none  [the longest x1 12 us: body(): lax.all_to_all(updated, 'freq', split_axis=3, concat_axis=1, tiled=True)]
    psum x1 -> x0, waiting for transfers between devices: 18 us -> none  [body(): model_re, model_im = lax.psum((model_re, model_im), 'rcv')]
  transfers between devices with their start and end apart: 3 -> 0, of which waited for: 3 -> 0; matrix products, arithmetic and copies ran while one was open for 1% -> 0% of each run, Pallas kernels for 0% -> 0%
where the time goes in v1:
time: 327 us
  Pallas kernels  320 us (98%)
  local copies, waits for them, and re-layouts  3.93 us (1%)
    pallas_call x1, Pallas kernels, body(): pl.pallas_call(partial(update_kernel, nx, nz, nchunk, rows, lines, norm),...  306 us
    pallas_call x1, Pallas kernels, body(): pl.pallas_call(partial(trace_kernel, rows, 32, math.sqrt(RCV / NF)), out_...  14.8 us

profile of v1, /device:TPU:0, one launch (start us, length us, event | category | flops | bytes accessed | tf_op | source)
XLA Modules:
  0.0 326.8 jit_solution(7405745824486436032)
XLA Ops:
  1.3 1.3 copy.12.pos
  2.6 0.8 mul.52
  3.4 1.2 cosine_convert_fusion
  4.7 0.1 copy.13.table
  4.8 1.7 copy.11
  6.5 305.5 %update.1 = bf16[4,8,128,2048]{3,2,1,0:T(8,128)(2,1)} custom-call(bf16[2,512,2048]{2,1,0:T(8,128)(2,1)} %bitcast.10, bf16[2,512,2048]{2,1,0:T(8,128)(2,1)} %bitcast.11, bf16[2,512,16]{2,1,0:T(8,128)(2,1)} %bitcast.12, f32[2,64]{1,0:T(2,128)} %wav.1, s32[8,1]{1,0:T(8,128)} %copy.12.pos, f32[1]{0:T(128)S(6)} %copy.15.step), custom_call_target="tpu_custom_call" | custom-call | tf_op jit(solution)/shard_map/update/pallas_call | solution.py:249
  312.1 14.8 %traces.1 = bf16[2048,2048]{1,0:T(8,128)(2,1)} custom-call(f32[1]{0:T(128)S(6)} %div.3.level, bf16[256,512]{1,0:T(8,128)(2,1)S(1)} %copy.13.table, bf16[32,128,2048]{2,1,0:T(8,128)(2,1)} %bitcast.9), custom_call_target="tpu_custom_call" | custom-call | tf_op jit(solution)/shard_map/traces/pallas_call | solution.py:287
  (2 shorter events, 0.0 us)

commit v2 on v1

--- a/solution.py
+++ b/solution.py
@@ -12,6 +12,8 @@
 RCV = 4096
 NT = 1024
 FC = 8
+BLOCK = 256
+LAG = 2
 MESH = pl.DeviceIdType.MESH
 
 
@@ -19,11 +21,30 @@
     return lax.broadcasted_iota(jnp.int32, shape, dim)
 
 
+def make_traces(u, table, lv, gain, rows, t_group, sparse, out):
+    groups, _, width = u.shape
+    part = 2 * FC
+    nt = table.shape[0]
+    for i in range(rows):
+        ui = u[:, i * part:(i + 1) * part, :].reshape(groups * part, width)
+        tr = jnp.dot(table[...], ui, preferred_element_type=jnp.float32) * gain
+        sparse[i] = (jnp.maximum(tr - lv, 0.0) + jnp.minimum(tr + lv, 0.0)).astype(jnp.bfloat16)
+    n = t_group * rows
+    dst, src = iota((n, n), 0), iota((n, n), 1)
+    perm = (src == (dst % rows) * t_group + dst // rows).astype(jnp.bfloat16)
+    for g in range(nt // t_group):
+        x = sparse[:, g * t_group:(g + 1) * t_group, :].reshape(n, width)
+        out[g * n:(g + 1) * n, :] = jnp.dot(
+            perm, x, preferred_element_type=jnp.float32
+        ).astype(jnp.bfloat16)
+
+
 def update_kernel(
-    nx, nz, nchunk, rows, lines, norm,
-    data, est, win, wav, pos, step, out,
-    down, est_p, upd, mod_mine, mod_other,
-    x_send, x_recv, c_send, c_recv, r_send, r_recv, l_send, l_recv, own_sem,
+    nx, nz, nchunk, rows, lines, norm, blocks, helped, gain, t_group,
+    data, est, win, wav, pos, step, level, table, out, given,
+    down, est_p, upd, mod_mine, mod_other, ubuf, sparse, made,
+    x_send, x_recv, c_send, c_recv, za_send, za_recv, zb_send, zb_recv,
+    zc_send, zc_recv, g_send, g_recv, own_sem, ubuf_sem,
 ):
     mx = lax.axis_index("shot")
     mz = lax.axis_index("freq")
@@ -65,16 +86,48 @@
             device_id={"rcv": 1 - mc}, device_id_type=MESH,
         )
 
-    def z_copy(src, slot, k, way):
-        send, recv = (r_send, r_recv) if way > 0 else (l_send, l_recv)
+    def w_of(way):
+        return 0 if way > 0 else 1
+
+    def last(z, way):
+        return z == (nz - 1 if way > 0 else 0)
+
+    def a_copy(src, slot, k, way):
         return pltpu.make_async_remote_copy(
-            src_ref=src, dst_ref=out.at[slot, k],
-            send_sem=send.at[slot, k], recv_sem=recv.at[slot, k],
+            src_ref=src, dst_ref=out.at[pl.ds(0, helped), slot, k],
+            send_sem=za_send.at[w_of(way), slot, k], recv_sem=za_recv.at[w_of(way), slot, k],
             device_id={"freq": mz + way}, device_id_type=MESH,
         )
 
+    def b_copy(src, slot, k, way):
+        return pltpu.make_async_remote_copy(
+            src_ref=src, dst_ref=out.at[pl.ds(helped, blocks - helped), slot, k],
+            send_sem=zb_send.at[w_of(way), slot, k], recv_sem=zb_recv.at[w_of(way), slot, k],
+            device_id={"freq": mz + way}, device_id_type=MESH,
+        )
+
+    def block_copy(slot, b, way):
+        piece = out.at[b, slot]
+        return pltpu.make_async_remote_copy(
+            src_ref=piece, dst_ref=piece,
+            send_sem=zc_send.at[w_of(way), slot, b], recv_sem=zc_recv.at[w_of(way), slot, b],
+            device_id={"freq": mz + way}, device_id_type=MESH,
+        )
+
+    def given_copy(b, way):
+        return pltpu.make_async_remote_copy(
+            src_ref=made.at[b], dst_ref=given.at[b],
+            send_sem=g_send.at[b], recv_sem=g_recv.at[b],
+            device_id={"freq": mz + way}, device_id_type=MESH,
+        )
+
+    a_own = lambda k: upd.at[k, pl.ds(0, helped)]
+    b_own = lambda k: upd.at[k, pl.ds(helped, blocks - helped)]
+    a_out = lambda slot, k: out.at[pl.ds(0, helped), slot, k]
+    b_out = lambda slot, k: out.at[pl.ds(helped, blocks - helped), slot, k]
+
     def own_copy(k):
-        return pltpu.make_async_copy(upd.at[k], out.at[mz, k], own_sem.at[k])
+        return pltpu.make_async_copy(upd.at[k], out.at[:, mz, k], own_sem.at[k])
 
     column = mc * width + iota((lines, width), 1)
     select = (column == pos[:, :]).astype(jnp.float32)
@@ -148,92 +201,197 @@
             [jnp.concatenate([e_re, e_im], axis=2), jnp.concatenate([e_im, -e_re], axis=2)], axis=1
         ).reshape(n, 2 * cols).astype(jnp.bfloat16)
         grad = jnp.dot(e, down[k].reshape(2 * cols, width), preferred_element_type=jnp.float32)
-        upd[k] = (est_p[k].astype(jnp.float32) - scale * (grad * norm)).astype(jnp.bfloat16)
+        new = (est_p[k].astype(jnp.float32) - scale * (grad * norm)).astype(jnp.bfloat16)
+        for b in range(blocks):
+            upd[k, b] = new[:, b * BLOCK:(b + 1) * BLOCK]
         own_copy(k).start()
-
-        @pl.when(mz < nz - 1)
-        def _():
-            z_copy(upd.at[k], mz, k, 1).start()
-
-        @pl.when(mz > 0)
-        def _():
-            z_copy(upd.at[k], mz, k, -1).start()
+        for way in (1, -1):
+            @pl.when(jnp.logical_not(last(mz, way)))
+            def _():
+                b_copy(b_own(k), mz, k, way).start()
+
+                if helped:
+                    @pl.when(jnp.logical_not(last(mz + way, way)))
+                    def _():
+                        a_copy(a_own(k), mz, k, way).start()
+
+    def near(k):
+        for way in (1, -1):
+            slot = mz - way
+
+            @pl.when((slot >= 0) & (slot < nz))
+            def _():
+                b_copy(b_out(slot, k), slot, k, way).wait_recv()
+
+                if helped:
+                    @pl.when(jnp.logical_not(last(mz, way)))
+                    def _():
+                        a_copy(a_out(slot, k), slot, k, way).wait_recv()
+
+                @pl.when(last(mz + way, way))
+                def _():
+                    b_copy(b_out(slot, k), slot, k, way).start()
 
     def step_of(k, carry):
         @pl.when(k < nchunk)
         def _():
             model(k)
 
-        @pl.when(k > 0)
+        @pl.when((k > 0) & (k <= nchunk))
         def _():
             update(k - 1)
 
-        return carry
-
-    lax.fori_loop(0, nchunk + 1, step_of, 0)
-
-    def hop(h, carry):
-        def one(k, carry):
+        @pl.when(k >= LAG)
+        def _():
+            near(k - LAG)
+
+        return carry
+
+    lax.fori_loop(0, nchunk + LAG, step_of, 0)
+
+    def own_done(k, carry):
+        own_copy(k).wait()
+        return carry
+
+    lax.fori_loop(0, nchunk, own_done, 0)
+
+    def hand_on(b, carry):
+        for way in (1, -1):
+            slot = mz - way
+            inside = (slot >= 0) & (slot < nz)
+            nxt = mz + way
+
+            @pl.when(inside & (nxt > 0) & (nxt < nz - 1))
+            def _():
+                block_copy(slot, b, way).start()
+
+        return carry
+
+    lax.fori_loop(0, blocks, hand_on, 0)
+
+    def far(h, carry):
+        def one(b, carry):
             for way in (1, -1):
                 slot = mz - way * h
+                nxt = mz + way
                 inside = (slot >= 0) & (slot < nz)
-                more = (mz + way >= 0) & (mz + way < nz)
-
-                @pl.when(inside)
+                at_end = last(mz, way)
+
+                @pl.when(inside & jnp.logical_not(at_end))
                 def _():
-                    here = out.at[slot, k]
-                    z_copy(here, slot, k, way).wait_recv()
-
-                @pl.when(inside & more)
+                    block_copy(slot, b, way).wait_recv()
+
+                    @pl.when(jnp.logical_not(last(nxt, way)) | (b >= helped))
+                    def _():
+                        block_copy(slot, b, way).start()
+
+                    if helped:
+                        @pl.when(last(nxt, way) & (b < helped) & last(slot, -way))
+                        def _():
+                            load = pltpu.make_async_copy(out.at[b], ubuf, ubuf_sem)
+                            load.start()
+                            load.wait()
+                            make_traces(
+                                ubuf.reshape(nz * nchunk, ubuf.shape[2], BLOCK), table, level[0],
+                                gain, rows, t_group, sparse, made.at[b],
+                            )
+                            given_copy(b, way).start()
+
+                @pl.when(inside & at_end & (b >= helped))
                 def _():
-                    z_copy(out.at[slot, k], slot, k, way).start()
+                    if not near_by:
+                        block_copy(slot, b, way).wait_recv()
 
             return carry
 
-        return lax.fori_loop(0, nchunk, one, carry)
-
-    lax.fori_loop(1, nz, hop, 0)
+        near_by = isinstance(h, int)
+        return lax.fori_loop(0, blocks, one, carry)
+
+    def end_chunk(k, carry):
+        for way in (1, -1):
+            slot = mz - 2 * way
+
+            @pl.when((slot >= 0) & (slot < nz) & last(mz, way))
+            def _():
+                b_copy(b_out(slot, k), slot, k, way).wait_recv()
+
+        return carry
+
+    if nz > 2:
+        lax.fori_loop(0, nchunk, end_chunk, 0)
+        far(2, 0)
+    lax.fori_loop(3, nz, far, 0)
+
+    if helped:
+        def take(b, carry):
+            for way in (1, -1):
+                @pl.when(last(mz, way))
+                def _():
+                    given_copy(b, way).wait_recv()
+
+                @pl.when(last(mz + way, way))
+                def _():
+                    given_copy(b, way).wait_send()
+
+            return carry
+
+        lax.fori_loop(0, helped, take, 0)
 
     def drain(k, carry):
         for d in range(1, nx):
             x_copy(d, k).wait_send()
         c_copy(k).wait_send()
-        own_copy(k).wait()
-
-        def hop_sent(h, carry):
+        for way in (1, -1):
+            nxt = mz + way
+
+            @pl.when(jnp.logical_not(last(mz, way)))
+            def _():
+                b_copy(b_own(k), mz, k, way).wait_send()
+
+                if helped:
+                    @pl.when(jnp.logical_not(last(nxt, way)))
+                    def _():
+                        a_copy(a_own(k), mz, k, way).wait_send()
+
+            slot = mz - way
+
+            @pl.when((slot >= 0) & (slot < nz) & last(nxt, way))
+            def _():
+                b_copy(b_own(k), slot, k, way).wait_send()
+
+        return carry
+
+    lax.fori_loop(0, nchunk, drain, 0)
+
+    def drain_far(h, carry):
+        def one(b, carry):
             for way in (1, -1):
                 slot = mz - way * h
-                inside = (slot >= 0) & (slot < nz)
-                more = (mz + way >= 0) & (mz + way < nz)
-
-                @pl.when(inside & more)
+                nxt = mz + way
+                inside = (slot >= 0) & (slot < nz) & (nxt >= 0) & (nxt < nz)
+                to_end = last(nxt, way)
+
+                @pl.when(inside & (jnp.logical_not(to_end) | ((b >= helped) & (h > 1))))
                 def _():
-                    z_copy(upd.at[k], slot, k, way).wait_send()
+                    block_copy(slot, b, way).wait_send()
 
             return carry
 
-        return lax.fori_loop(0, nz, hop_sent, carry)
-
-    lax.fori_loop(0, nchunk, drain, 0)
-
-
-def trace_kernel(rows, t_group, gain, level, table, u, out, sparse):
-    groups, _, width = u.shape
-    part = 2 * FC
-    nt = table.shape[0]
-    lv = level[0]
-    for i in range(rows):
-        ui = u[:, i * part:(i + 1) * part, :].reshape(groups * part, width)
-        tr = jnp.dot(table[...], ui, preferred_element_type=jnp.float32) * gain
-        sparse[i] = (jnp.maximum(tr - lv, 0.0) + jnp.minimum(tr + lv, 0.0)).astype(jnp.bfloat16)
-    n = t_group * rows
-    dst, src = iota((n, n), 0), iota((n, n), 1)
-    perm = (src == (dst % rows) * t_group + dst // rows).astype(jnp.bfloat16)
-    for g in range(nt // t_group):
-        x = sparse[:, g * t_group:(g + 1) * t_group, :].reshape(n, width)
-        out[g * n:(g + 1) * n, :] = jnp.dot(
-            perm, x, preferred_element_type=jnp.float32
-        ).astype(jnp.bfloat16)
+        return lax.fori_loop(0, blocks, one, carry)
+
+    lax.fori_loop(1, nz, drain_far, 0)
+
+
+def trace_kernel(rows, t_group, gain, helped, level, taken, table, u, given, out, sparse):
+    ready = (pl.program_id(0) < helped) & (taken[0] > 0)
+
+    @pl.when(ready)
+    def _():
+        out[...] = given[...]
+
+    @pl.when(jnp.logical_not(ready))
+    def _():
+        make_traces(u, table, level[0], gain, rows, t_group, sparse, out)
 
 
 def body(nx, nz, data, estimate, window_data, wavelet, positions, bins, threshold, step):
@@ -243,28 +401,55 @@
     nchunk = nf // FC
     norm = 1.0 / math.sqrt(shots * RCV)
     fi, cols = FC * rows, nx * FC * lines
+    mz = lax.axis_index("freq")
+    nt = NT // nz
+    blocks, groups = width // BLOCK, nz * nchunk
+    helped = blocks // 2 if nz >= 4 else 0
+    held = max(helped, 1)
+    gain, t_group = math.sqrt(RCV / NF), 32
+    level = threshold.astype(jnp.float32) / 64.0
+
+    def table_of(z):
+        times = z * nt + lax.iota(jnp.int32, nt)
+        phase = times[:, None] * bins[None, :] % NT
+        angle = 2.0 * math.pi / NT * phase.astype(jnp.float32)
+        table = jnp.stack([jnp.cos(angle), -jnp.sin(angle)], axis=1).astype(jnp.bfloat16)
+        table = table.reshape(nt, 2, groups, FC).transpose(0, 2, 1, 3)
+        return table.reshape(nt, 2 * nz * nf)
+
     vmem = pl.BlockSpec(memory_space=pltpu.VMEM)
     smem = pl.BlockSpec(memory_space=pltpu.SMEM)
+    hbm = pl.BlockSpec(memory_space=pl.ANY)
     dma = pltpu.SemaphoreType.DMA
-    spectra = pl.pallas_call(
-        partial(update_kernel, nx, nz, nchunk, rows, lines, norm),
-        out_shape=jax.ShapeDtypeStruct((nz, nchunk, 2 * fi, width), jnp.bfloat16),
-        in_specs=[vmem, vmem, vmem, smem, vmem, smem],
-        out_specs=pl.BlockSpec(memory_space=pl.ANY),
+    spectra, given = pl.pallas_call(
+        partial(
+            update_kernel, nx, nz, nchunk, rows, lines, norm, blocks, helped, gain, t_group
+        ),
+        out_shape=(
+            jax.ShapeDtypeStruct((blocks, nz, nchunk, 2 * fi, BLOCK), jnp.bfloat16),
+            jax.ShapeDtypeStruct((held, nt * rows, BLOCK), jnp.bfloat16),
+        ),
+        in_specs=[vmem, vmem, vmem, smem, vmem, smem, smem, vmem],
+        out_specs=(hbm, hbm),
         scratch_shapes=[
             pltpu.VMEM((nchunk, 2, cols, width), jnp.bfloat16),
             pltpu.VMEM((nchunk, 2 * fi, width), jnp.bfloat16),
-            pltpu.VMEM((nchunk, 2 * fi, width), jnp.bfloat16),
+            pltpu.VMEM((nchunk, blocks, 2 * fi, BLOCK), jnp.bfloat16),
             pltpu.VMEM((nchunk, 2, rows, FC, cols), jnp.float32),
             pltpu.VMEM((nchunk, 2, rows, FC, cols), jnp.float32),
+            pltpu.VMEM((nz, nchunk, 2 * fi, BLOCK), jnp.bfloat16),
+            pltpu.VMEM((rows, nt, BLOCK), jnp.bfloat16),
+            pltpu.VMEM((held, nt * rows, BLOCK), jnp.bfloat16),
             dma((nx, nchunk)), dma((nx, nchunk)),
             dma((nchunk,)), dma((nchunk,)),
-            dma((nz, nchunk)), dma((nz, nchunk)),
-            dma((nz, nchunk)), dma((nz, nchunk)),
-            dma((nchunk,)),
+            dma((2, nz, nchunk)), dma((2, nz, nchunk)),
+            dma((2, nz, nchunk)), dma((2, nz, nchunk)),
+            dma((2, nz, blocks)), dma((2, nz, blocks)),
+            dma((held,)), dma((held,)),
+            dma((nchunk,)), dma,
         ],
         compiler_params=pltpu.CompilerParams(
-            collective_id=0, has_side_effects=True, vmem_limit_bytes=56 << 20
+            collective_id=0, has_side_effects=True, vmem_limit_bytes=58 << 20
         ),
         name="update",
     )(
@@ -274,30 +459,28 @@
         wavelet,
         positions[:, None],
         step,
+        level,
+        table_of(jnp.where(mz < nz // 2, 0, nz - 1)),
     )
-    nt = NT // nz
-    times = lax.axis_index("freq") * nt + lax.iota(jnp.int32, nt)
-    phase = times[:, None] * bins[None, :] % NT
-    angle = 2.0 * math.pi / NT * phase.astype(jnp.float32)
-    table = jnp.stack([jnp.cos(angle), -jnp.sin(angle)], axis=1).astype(jnp.bfloat16)
-    table = table.reshape(nt, 2, nz * nchunk, FC).transpose(0, 2, 1, 3).reshape(nt, 2 * nz * nf)
-    level = threshold.astype(jnp.float32) / 64.0
-    block = 256
-    groups = nz * nchunk
+    taken = ((mz == 0) | (mz == nz - 1)).astype(jnp.int32)[None]
     traces = pl.pallas_call(
-        partial(trace_kernel, rows, 32, math.sqrt(RCV / NF)),
+        partial(trace_kernel, rows, t_group, gain, helped),
         out_shape=jax.ShapeDtypeStruct((nt * rows, width), jnp.bfloat16),
-        grid=(width // block,),
+        grid=(blocks,),
         in_specs=[
             smem,
+            smem,
             pl.BlockSpec((nt, 2 * nz * nf), lambda j: (0, 0)),
-            pl.BlockSpec((groups, 2 * fi, block), lambda j: (0, 0, j)),
+            pl.BlockSpec((None, groups, 2 * fi, BLOCK), lambda j: (j, 0, 0, 0)),
+            pl.BlockSpec(
+                (None, nt * rows, BLOCK), lambda j: (jnp.minimum(j, held - 1), 0, 0)
+            ),
         ],
-        out_specs=pl.BlockSpec((nt * rows, block), lambda j: (0, j)),
-        scratch_shapes=[pltpu.VMEM((rows, nt, block), jnp.bfloat16)],
+        out_specs=pl.BlockSpec((nt * rows, BLOCK), lambda j: (0, j)),
+        scratch_shapes=[pltpu.VMEM((rows, nt, BLOCK), jnp.bfloat16)],
         compiler_params=pltpu.CompilerParams(vmem_limit_bytes=40 << 20),
         name="traces",
-    )(level, table, spectra.reshape(groups, 2 * fi, width))
+    )(level, taken, table_of(mz), spectra.reshape(blocks, groups, 2 * fi, BLOCK), given)
     return traces.reshape(nt, rows, width)
 
 

time: 327 us -> 304 us (0.930)
  Pallas kernels: 320 us -> 293 us
    pallas_call x2, Pallas kernels: 320 us -> 293 us  [the longest x1 279 us: body(): pl.pallas_call(partial(update_kernel, nx, nz, nchunk, rows, lines, norm,...]
where the time goes in v2:
time: 304 us; the launch traced here: 303 us
  Pallas kernels  293 us (96%)
  local copies, waits for them, and re-layouts  6.96 us (2%)
    pallas_call x1, Pallas kernels, body(): pl.pallas_call(partial(update_kernel, nx, nz, nchunk, rows, lines, norm,...  279 us
    pallas_call x1, Pallas kernels, body(): pl.pallas_call(partial(trace_kernel, rows, t_group, gain, helped), out_sh...  13.3 us

profile of v2, /device:TPU:0, one launch (start us, length us, event | category | flops | bytes accessed | tf_op | source)
XLA Modules:
  0.0 303.4 jit_solution(14968776447122543540)
XLA Ops:
  1.3 1.3 copy.12.pos
  2.6 0.8 mul.92
  3.4 1.7 copy.11
  5.1 2.3 cosine_convert_fusion
  7.5 0.1 copy.14.table
  7.6 0.8 copy.13.table
  8.5 279.5 %update.1 = (bf16[8,4,8,128,256]{4,3,2,1,0:T(8,128)(2,1)}, bf16[4,2048,256]{2,1,0:T(8,128)(2,1)}) custom-call(bf16[2,512,2048]{2,1,0:T(8,128)(2,1)} %bitcast.14, bf16[2,512,2048]{2,1,0:T(8,128)(2,1)} %bitcast.15, bf16[2,512,16]{2,1,0:T(8,128)(2,1)} %bitcast.16, f32[2,64]{1,0:T(2,128)} %wav.1, s32[8,1]{1,0:T(8,128)} %copy.12.pos, f32[1]{0:T(128)S(6)} %copy.16.step, ...), custom_call_target="tpu_custom_call" | custom-call | tf_op jit(solution)/shard_map/update/pallas_call | solution.py:424
  287.9 0.0 copy-start
  288.0 2.2 copy-done
  290.1 13.3 %traces.1 = bf16[2048,2048]{1,0:T(8,128)(2,1)} custom-call(f32[1]{0:T(128)S(6)} %div.3.level, s32[1]{0:T(128)} %bitcast.taken, bf16[256,512]{1,0:T(8,128)(2,1)S(1)} %copy.14.table, bf16[8,32,128,256]{3,2,1,0:T(8,128)(2,1)} %bitcast.13, bf16[4,2048,256]{2,1,0:T(8,128)(2,1)S(1)} %copy-done), custom_call_target="tpu_custom_call" | custom-call | tf_op jit(solution)/shard_map/traces/pallas_call | solution.py:466
  (3 shorter events, 0.1 us)
Async XLA Ops:
  287.9 2.2 copy-start

commit v3 on v2

--- a/solution.py
+++ b/solution.py
@@ -13,7 +13,7 @@
 NT = 1024
 FC = 8
 BLOCK = 256
-LAG = 2
+LAG = 1
 MESH = pl.DeviceIdType.MESH
 
 
@@ -236,10 +236,7 @@
         @pl.when(k < nchunk)
         def _():
             model(k)
-
-        @pl.when((k > 0) & (k <= nchunk))
-        def _():
-            update(k - 1)
+            update(k)
 
         @pl.when(k >= LAG)
         def _():
@@ -478,7 +475,7 @@
         ],
         out_specs=pl.BlockSpec((nt * rows, BLOCK), lambda j: (0, j)),
         scratch_shapes=[pltpu.VMEM((rows, nt, BLOCK), jnp.bfloat16)],
-        compiler_params=pltpu.CompilerParams(vmem_limit_bytes=40 << 20),
+        compiler_params=pltpu.CompilerParams(vmem_limit_bytes=60 << 20),
         name="traces",
     )(level, taken, table_of(mz), spectra.reshape(blocks, groups, 2 * fi, BLOCK), given)
     return traces.reshape(nt, rows, width)

time: 304 us -> 296 us (0.974)
  Pallas kernels: 293 us -> 287 us
    pallas_call x1, Pallas kernels: 279 us -> 272 us  [body(): pl.pallas_call(partial(update_kernel, nx, nz, nchunk, rows, lines, norm,...]
where the time goes in v3:
time: 296 us
  Pallas kernels  287 us (97%)
  local copies, waits for them, and re-layouts  5.48 us (2%)
    pallas_call x1, Pallas kernels, body(): pl.pallas_call(partial(update_kernel, nx, nz, nchunk, rows, lines, norm,...  272 us
    pallas_call x1, Pallas kernels, body(): pl.pallas_call(partial(trace_kernel, rows, t_group, gain, helped), out_sh...  14.1 us

profile of v3, /device:TPU:0, one launch (start us, length us, event | category | flops | bytes accessed | tf_op | source)
XLA Modules:
  0.0 295.7 jit_solution(3647547392615447733)
XLA Ops:
  1.3 1.3 copy.12.pos
  2.6 0.8 mul.92
  3.4 1.7 copy.11
  5.1 2.3 cosine_convert_fusion
  7.5 0.8 copy.14.table
  8.3 0.8 copy.13.table
  9.2 272.4 %update.1 = (bf16[8,4,8,128,256]{4,3,2,1,0:T(8,128)(2,1)}, bf16[4,2048,256]{2,1,0:T(8,128)(2,1)}) custom-call(bf16[2,512,2048]{2,1,0:T(8,128)(2,1)} %bitcast.14, bf16[2,512,2048]{2,1,0:T(8,128)(2,1)} %bitcast.15, bf16[2,512,16]{2,1,0:T(8,128)(2,1)} %bitcast.16, f32[2,64]{1,0:T(2,128)} %wav.1, s32[8,1]{1,0:T(8,128)} %copy.12.pos, f32[1]{0:T(128)S(6)} %copy.16.step, ...), custom_call_target="tpu_custom_call" | custom-call | tf_op jit(solution)/shard_map/update/pallas_call | solution.py:421
  281.6 14.1 %traces.1 = bf16[2048,2048]{1,0:T(8,128)(2,1)} custom-call(f32[1]{0:T(128)S(6)} %div.3.level, s32[1]{0:T(128)} %bitcast.taken, bf16[256,512]{1,0:T(8,128)(2,1)} %copy.14.table, bf16[8,32,128,256]{3,2,1,0:T(8,128)(2,1)} %bitcast.13, bf16[4,2048,256]{2,1,0:T(8,128)(2,1)} %get-tuple-element.8.given), custom_call_target="tpu_custom_call" | custom-call | tf_op jit(solution)/shard_map/traces/pallas_call | solution.py:463
  (3 shorter events, 0.1 us)

commit v4 on v3

--- a/solution.py
+++ b/solution.py
@@ -401,7 +401,7 @@
     mz = lax.axis_index("freq")
     nt = NT // nz
     blocks, groups = width // BLOCK, nz * nchunk
-    helped = blocks // 2 if nz >= 4 else 0
+    helped = 3 * blocks // 8 if nz >= 4 else 0
     held = max(helped, 1)
     gain, t_group = math.sqrt(RCV / NF), 32
     level = threshold.astype(jnp.float32) / 64.0

time: 296 us -> 293 us (0.990)
  Pallas kernels: 287 us -> 284 us
where the time goes in v4:
time: 293 us
  Pallas kernels  284 us (97%)
  local copies, waits for them, and re-layouts  5.5 us (2%)
    pallas_call x1, Pallas kernels, body(): pl.pallas_call(partial(update_kernel, nx, nz, nchunk, rows, lines, norm,...  270 us
    pallas_call x1, Pallas kernels, body(): pl.pallas_call(partial(trace_kernel, rows, t_group, gain, helped), out_sh...  14 us

profile of v4, /device:TPU:0, one launch (start us, length us, event | category | flops | bytes accessed | tf_op | source)
XLA Modules:
  0.0 293.0 jit_solution(15723665657515301010)
XLA Ops:
  1.3 1.3 copy.12.pos
  2.6 0.8 mul.92
  3.4 1.7 copy.11
  5.1 2.3 cosine_convert_fusion
  7.5 0.8 copy.14.table
  8.3 0.9 copy.13.table
  9.2 269.8 %update.1 = (bf16[8,4,8,128,256]{4,3,2,1,0:T(8,128)(2,1)}, bf16[3,2048,256]{2,1,0:T(8,128)(2,1)}) custom-call(bf16[2,512,2048]{2,1,0:T(8,128)(2,1)} %bitcast.14, bf16[2,512,2048]{2,1,0:T(8,128)(2,1)} %bitcast.15, bf16[2,512,16]{2,1,0:T(8,128)(2,1)} %bitcast.16, f32[2,64]{1,0:T(2,128)} %wav.1, s32[8,1]{1,0:T(8,128)} %copy.12.pos, f32[1]{0:T(128)S(6)} %copy.16.step, ...), custom_call_target="tpu_custom_call" | custom-call | tf_op jit(solution)/shard_map/update/pallas_call | solution.py:421
  279.0 14.0 %traces.1 = bf16[2048,2048]{1,0:T(8,128)(2,1)} custom-call(f32[1]{0:T(128)S(6)} %div.3.level, s32[1]{0:T(128)} %bitcast.taken, bf16[256,512]{1,0:T(8,128)(2,1)} %copy.14.table, bf16[8,32,128,256]{3,2,1,0:T(8,128)(2,1)} %bitcast.13, bf16[3,2048,256]{2,1,0:T(8,128)(2,1)} %get-tuple-element.8.given), custom_call_target="tpu_custom_call" | custom-call | tf_op jit(solution)/shard_map/traces/pallas_call | solution.py:463
  (3 shorter events, 0.1 us)
